TPU v7x, 256 devices: a whole 4x4x8 slice. The times are simulated.
256 devices in a mesh: energy: 64 (over z, y_lo, x), cuts: 4 (over y_hi, core).
Axes of the slice: x: 4, y: 4 (y_hi: 2, y_lo: 2; y = y_hi * 2 + y_lo), z: 8, core: 2. Of those that a mesh axis runs over, the one named last changes fastest.
Arguments:
- lesser: bfloat16 [128, 4, 2, 512, 512], P('energy', 'cuts'), may hold values from -6 to 6
- greater: bfloat16 [128, 4, 2, 512, 512], P('energy', 'cuts'), may hold values from -6 to 6
- couplings: bfloat16 [4, 3, 512, 512], P('cuts'), may hold values from -0.25 to 0.25
- rim_couple: bfloat16 [4, 2, 128, 128], P('cuts'), may hold values from -0.5 to 0.5
- bose_factor: float32 [3], replicated, may hold values from 0.05 to 2
- offsets: int32 [3], replicated, may hold values from 1 to 2, as said below
- pattern: int32 [4, 3], replicated, may hold values from 0 to 1, as said below
Outputs:
- sigma_lesser: bfloat16 [128, 4, 2, 512, 512], P('energy', 'cuts')
- sigma_retarded: bfloat16 [128, 4, 2, 512, 512], P('energy', 'cuts')
Inputs may be any that keep to these rules, and one draw needn't show every extreme that they name: `offsets`: one mode's shift is exactly 2. `pattern`: each block couples to 1 to 3 modes. In every draw one block couples to all 3 modes and the other block of its aligned pair (blocks 2i and 2i + 1) to exactly one.
All inputs are finite; a program needn't handle non-finite values.
Results may differ from a plain program's by a relative error of at most 0.0057.
Values may be sent and summed in bfloat16 or wider, within the bound.
No kernel may reach another device: no remote copies, remote signals or barrier semaphores. Data moves between devices by JAX's collectives and lax.ppermute only.
A program may use at most 128 MiB of HBM per device.

v0:
```python
import jax
import jax.numpy as jnp
from jax import lax
from jax.sharding import PartitionSpec as P


def passed_along(x, axis, by):
    length = lax.axis_size(axis)
    pairs = [(i, i + by) for i in range(length) if 0 <= i + by < length]
    return lax.ppermute(x, axis, pairs)


def extended(cells, sides, width):
    for axis, dim in sides:
        count = lax.axis_size(axis)
        ends = count - 1
        head = lax.slice_in_dim(cells, 0, width, axis=dim)
        tail = lax.slice_in_dim(cells, cells.shape[dim] - width, cells.shape[dim], axis=dim)
        cells = jnp.concatenate(
            [
                lax.ppermute(tail, axis, [(i, (i + 1) % count) for i in range(ends)]),
                cells,
                lax.ppermute(head, axis, [((i + 1) % count, i) for i in range(ends)]),
            ],
            axis=dim,
        )
    return cells


def blend_shift(padded, energy_rows, shift, weight):
    ahead_green = lax.dynamic_slice_in_dim(padded, energy_rows + shift, energy_rows, 0)
    behind = lax.dynamic_slice_in_dim(padded, energy_rows - shift, energy_rows, 0)
    lead_weight = jnp.stack([weight + 1.0, weight])
    trail_weight = jnp.stack([weight, weight + 1.0])
    mixed_green = lead_weight[None, :, None, None, None] * ahead_green.astype(
        jnp.float32
    ) + trail_weight[None, :, None, None, None] * behind.astype(jnp.float32)
    return mixed_green.astype(jnp.bfloat16)


def sandwich(matrix, mixed_green):
    left_product = jnp.einsum(
        "ij,etpjk->etpik", matrix, mixed_green, preferred_element_type=jnp.float32
    ).astype(jnp.bfloat16)
    return jnp.einsum("etpij,kj->etpik", left_product, matrix, preferred_element_type=jnp.float32)


def body(lesser, greater, couplings, rim_couple, bose_factor, offsets, pattern):
    energy_rows = lesser.shape[0]
    orbitals = lesser.shape[3]
    rim_width = rim_couple.shape[2]
    mode_count = couplings.shape[1]
    green_pair = jnp.concatenate([lesser, greater], 1)
    from_low = passed_along(
        green_pair[:, :, :, orbitals - rim_width :, orbitals - rim_width :], "cuts", 1
    )
    from_high = passed_along(green_pair[:, :, :, :rim_width, :rim_width], "cuts", -1)
    couple = rim_couple[0]
    low_term = sandwich(couple[0], from_low)
    high_term = sandwich(couple[1], from_high)
    padded = extended(green_pair, (("energy", 0),), energy_rows)
    own_block = lax.axis_index("cuts")
    mode_flags = lax.dynamic_index_in_dim(pattern, own_block, 0, keepdims=False)
    mode_couplings = couplings[0]

    def mode_term(mode_index):
        mixed_green = blend_shift(padded, energy_rows, offsets[mode_index], bose_factor[mode_index])
        matrix = lax.dynamic_index_in_dim(mode_couplings, mode_index, 0, keepdims=False)
        return sandwich(matrix, mixed_green)

    def unchanged(running):
        return running

    accumulated = jnp.zeros(green_pair.shape, jnp.float32)
    for mode_index in range(mode_count):

        def add_mode(running, chosen=mode_index):
            return running + mode_term(chosen)

        accumulated = lax.cond(mode_flags[mode_index] > 0, add_mode, unchanged, accumulated)
    accumulated = accumulated.at[:, :, :, :rim_width, :rim_width].add(low_term)
    accumulated = accumulated.at[:, :, :, orbitals - rim_width :, orbitals - rim_width :].add(
        high_term
    )
    lesser_part = accumulated[:, 0]
    retarded = 0.5 * (accumulated[:, 1] - accumulated[:, 0])
    return (lesser_part[:, None].astype(jnp.bfloat16), retarded[:, None].astype(jnp.bfloat16))


def solution(mesh):
    return jax.shard_map(
        body,
        mesh=mesh,
        in_specs=(
            P("energy", "cuts", None, None, None),
            P("energy", "cuts", None, None, None),
            P("cuts", None, None, None),
            P("cuts", None, None, None),
            P(),
            P(),
            P(),
        ),
        out_specs=(P("energy", "cuts", None, None, None), P("energy", "cuts", None, None, None)),
        check_vma=False,
    )
```

profile of v0, /device:TPU:144, one launch (start us, length us, event | category | flops | bytes accessed | tf_op | source)
XLA Modules:
  0.0 178.4 jit_solution(5268781628275176267)
XLA Ops:
  0.6 0.0 copy-start
  0.6 3.1 %constant_dynamic-update-slice_fusion.1 = bf16[2,2,2,512,512]{4,3,2,1,0:T(8,128)(2,1)} fusion(bf16[2,1,2,512,512]{4,3,2,1,0:T(8,128)(2,1)} %param.17), kind=kLoop, calls=%fused_computation.64 | loop fusion | bytes 4194304
  3.7 3.1 %constant_dynamic-update-slice_fusion = bf16[2,2,2,512,512]{4,3,2,1,0:T(8,128)(2,1)} fusion(bf16[2,2,2,512,512]{4,3,2,1,0:T(8,128)(2,1)} %constant_dynamic-update-slice_fusion.1, bf16[2,1,2,512,512]{4,3,2,1,0:T(8,128)(2,1)} %param.18), kind=kLoop, calls=%fused_computation.63 | loop fusion | bytes 4194304 | tf_op jit(solution)/shard_map/concatenate | solution.py:53
  6.8 4.9 %collective-permute-start.1 = (bf16[2,2,2,512,512]{4,3,2,1,0:T(8,128)(2,1)}, bf16[2,2,2,512,512]{4,3,2,1,0:T(8,128)(2,1)}, u32[]{:S(2)}, u32[]{:S(2)}) collective-permute-start(bf16[2,2,2,512,512]{4,3,2,1,0:T(8,128)(2,1)} %constant_dynamic-update-slice_fusion), channel_id=1, source_target_pairs={{4,0},{8,4},{12,8},{16,12},{20,16},{24,20},{28,24},{32,28},{36,32}... | collective-permute-start | bytes 12582920 | tf_op jit(solution)/shard_map/ppermute | solution.py:23
  11.8 1.9 %collective-permute-start = (bf16[2,2,2,512,512]{4,3,2,1,0:T(8,128)(2,1)}, bf16[2,2,2,512,512]{4,3,2,1,0:T(8,128)(2,1)}, u32[]{:S(2)}, u32[]{:S(2)}) collective-permute-start(bf16[2,2,2,512,512]{4,3,2,1,0:T(8,128)(2,1)} %constant_dynamic-update-slice_fusion), channel_id=1, source_target_pairs={{0,4},{4,8},{8,12},{12,16},{16,20},{20,24},{24,28},{28,32},{32,36}... | collective-permute-start | bytes 12582920 | tf_op jit(solution)/shard_map/ppermute | solution.py:21
  13.7 1.1 fusion.72
  14.8 1.9 %collective-permute-start.3 = (bf16[2,2,2,128,128]{4,3,2,1,0:T(8,128)(2,1)S(1)}, bf16[2,2,2,128,128]{4,3,2,1,0:T(8,128)(2,1)S(1)}, u32[]{:S(2)}, u32[]{:S(2)}) collective-permute-start(bf16[2,2,2,128,128]{4,3,2,1,0:T(8,128)(2,1)S(1)} %get-tuple-element.91), channel_id=1, source_target_pairs={{1,0},{2,1},{3,2},{5,4},{6,5},{7,6},{9,8},{10,9},{11,10},{13,12},{... | collective-permute-start | bytes 786440 | tf_op jit(solution)/shard_map/ppermute | solution.py:10
  16.7 2.4 %collective-permute-start.2 = (bf16[2,2,2,128,128]{4,3,2,1,0:T(8,128)(2,1)S(1)}, bf16[2,2,2,128,128]{4,3,2,1,0:T(8,128)(2,1)S(1)}, u32[]{:S(2)}, u32[]{:S(2)}) collective-permute-start(bf16[2,2,2,128,128]{4,3,2,1,0:T(8,128)(2,1)S(1)} %get-tuple-element.92), channel_id=1, source_target_pairs={{0,1},{1,2},{2,3},{4,5},{5,6},{6,7},{8,9},{9,10},{10,11},{12,13},{... | collective-permute-start | bytes 786440 | tf_op jit(solution)/shard_map/ppermute | solution.py:10
  19.1 0.0 copy-done
  19.2 0.7 fusion.73
  21.8 0.0 copy-start.2
  21.8 0.0 copy-start.3
  21.8 0.0 copy-start.4
  21.9 80.0 %collective-permute-done.1 = bf16[2,2,2,512,512]{4,3,2,1,0:T(8,128)(2,1)} collective-permute-done((bf16[2,2,2,512,512]{4,3,2,1,0:T(8,128)(2,1)}, bf16[2,2,2,512,512]{4,3,2,1,0:T(8,128)(2,1)}, u32[]{:S(2)}, u32[]{:S(2)}) %collective-permute-start.1) | collective-permute-done | bytes 4194336 | tf_op jit(solution)/shard_map/ppermute | solution.py:23
  101.9 8.4 %collective-permute-done = bf16[2,2,2,512,512]{4,3,2,1,0:T(8,128)(2,1)} collective-permute-done((bf16[2,2,2,512,512]{4,3,2,1,0:T(8,128)(2,1)}, bf16[2,2,2,512,512]{4,3,2,1,0:T(8,128)(2,1)}, u32[]{:S(2)}, u32[]{:S(2)}) %collective-permute-start) | collective-permute-done | bytes 4194336 | tf_op jit(solution)/shard_map/ppermute | solution.py:21
  110.3 10.5 %pad_maximum_fusion.6 = bf16[6,2,2,512,512]{4,3,2,1,0:T(8,128)(2,1)} fusion(bf16[2,2,2,512,512]{4,3,2,1,0:T(8,128)(2,1)} %collective-permute-done.1, bf16[2,2,2,512,512]{4,3,2,1,0:T(8,128)(2,1)} %constant_dynamic-update-slice_fusion, bf16[2,2,2,512,512]{4,3,2,1,0:T(8,128)(2,1)} %collective-permute-done), kind=kLoop, calls=%fused_computation.44 | loop fusion | flops 12582912 | bytes 25165824 | tf_op jit(solution)/shard_map/concatenate | solution.py:19
  120.8 0.0 copy-done.2
  120.8 0.0 copy-done.3
  120.8 0.0 copy-done.4
  120.8 11.8 %conditional.3 = (f32[2,2,2,512,512]{4,3,2,1,0:T(8,128)}) conditional(s32[]{:T(128)} %bitcast.26, () %tuple.44, (f32[3]{0:T(128)S(1)}, s32[3]{0:T(128)S(1)}, bf16[6,2,2,512,512]{4,3,2,1,0:T(8,128)(2,1)}, bf16[3,512,512]{2,1,0:T(8,128)(2,1)S(1)}) %tuple.67), branch_computations={%region_0.1_spmd, %region_1.2_spmd} | conditional | flops 4309647360 | bytes 17826960 | solution.py:80
  121.0 0.1 pad_maximum_fusion
  121.1 11.5 %fusion.1 = f32[2,2,2,512,512]{4,3,2,1,0:T(8,128)} fusion(bf16[6,2,2,512,512]{4,3,2,1,0:T(8,128)(2,1)} %get-tuple-element.70, s32[]{:T(128)S(6)} %select_n.20, f32[2]{0:T(128)S(1)} %get-tuple-element.86, s32[]{:T(128)S(6)} %select_n.19, f32[2]{0:T(128)S(1)} %get-tuple-element.85, bf16[3,512,512]{2,1,0:T(8,128)(2,1)S(1)} %get-tuple-element.72), kind=kOutput, calls=%fused_computation.2 | convolution fusion | flops 4309647360 | bytes 17826824 | tf_op jit(solution)/shard_map/cond/branch_1_fun/etpij,kj->etpik/dot_general | solution.py:45
  132.7 15.7 %conditional.4 = (f32[2,2,2,512,512]{4,3,2,1,0:T(8,128)}) conditional(s32[]{:T(128)} %bitcast.25, f32[2,2,2,512,512]{4,3,2,1,0:T(8,128)} %get-tuple-element.96, (f32[3]{0:T(128)S(1)}, s32[3]{0:T(128)S(1)}, bf16[6,2,2,512,512]{4,3,2,1,0:T(8,128)(2,1)}, bf16[3,512,512]{2,1,0:T(8,128)(2,1)S(1)}, f32[2,2,2,512,512]{4,3,2,1,0:T(8,128)}) %tuple.68), branch_computations={%region_2.3_spmd, %region_3.4_spmd} | conditional | flops 4311744512 | bytes 26215584 | solution.py:80
  132.7 0.6 slice.122
  135.8 0.6 slice.121
  137.1 0.7 pad_maximum_fusion.2
  137.8 10.6 %fusion.22 = f32[2,2,2,512,512]{4,3,2,1,0:T(8,128)} fusion(f32[2,2,2,512,512]{4,3,2,1,0:T(8,128)} %get-tuple-element.73, bf16[6,2,2,512,512]{4,3,2,1,0:T(8,128)(2,1)} %get-tuple-element.75, s32[]{:T(128)S(6)} %select_n.22, f32[2]{0:T(128)S(1)} %get-tuple-element.88, s32[]{:T(128)S(6)} %select_n.21, f32[2]{0:T(128)S(1)} %get-tuple-element.87, ...), kind=kOutput, calls=%fused_computation.23 | convolution fusion | flops 4311744512 | bytes 26215432 | tf_op jit(solution)/shard_map/cond/branch_1_fun/etpij,kj->etpik/dot_general | solution.py:45
  148.4 0.0 copy-start.1
  148.4 15.7 %conditional.5 = (f32[2,2,2,512,512]{4,3,2,1,0:T(8,128)}) conditional(s32[]{:T(128)} %bitcast.24, f32[2,2,2,512,512]{4,3,2,1,0:T(8,128)} %get-tuple-element.97, (f32[3]{0:T(128)S(1)}, s32[3]{0:T(128)S(1)}, bf16[6,2,2,512,512]{4,3,2,1,0:T(8,128)(2,1)}, bf16[3,512,512]{2,1,0:T(8,128)(2,1)S(1)}, f32[2,2,2,512,512]{4,3,2,1,0:T(8,128)}) %tuple.69), branch_computations={%region_4.5_spmd, %region_5.6_spmd} | conditional | flops 4311744512 | bytes 26215584 | solution.py:80
  148.4 0.6 slice.124
  151.6 0.6 slice.123
  152.8 0.7 pad_maximum_fusion.4
  153.5 10.6 %fusion.39 = f32[2,2,2,512,512]{4,3,2,1,0:T(8,128)} fusion(f32[2,2,2,512,512]{4,3,2,1,0:T(8,128)} %get-tuple-element.78, bf16[6,2,2,512,512]{4,3,2,1,0:T(8,128)(2,1)} %get-tuple-element.80, s32[]{:T(128)S(6)} %select_n.24, f32[2]{0:T(128)S(1)} %get-tuple-element.90, s32[]{:T(128)S(6)} %select_n.23, f32[2]{0:T(128)S(1)} %get-tuple-element.89, ...), kind=kOutput, calls=%fused_computation.38 | convolution fusion | flops 4311744512 | bytes 26215432 | tf_op jit(solution)/shard_map/cond/branch_1_fun/etpij,kj->etpik/dot_general | solution.py:45
  164.1 0.0 collective-permute-done.2
  164.1 0.0 copy-done.1
  164.1 2.3 %fusion.55 = f32[2,2,2,512,512]{4,3,2,1,0:T(8,128)} fusion(f32[2,2,2,512,512]{4,3,2,1,0:T(8,128)} %get-tuple-element.98, bf16[2,2,2,128,128]{4,3,2,1,0:T(8,128)(2,1)S(1)} %collective-permute-done.2, bf16[1,2,128,128]{3,2,1,0:T(8,128)(2,1)S(1)} %copy-done.1), kind=kOutput, calls=%fused_computation.58 | convolution fusion | flops 67371008 | bytes 1376256 | tf_op jit(solution)/shard_map/etpij,kj->etpik/dot_general | solution.py:45
  166.4 0.0 collective-permute-done.3
  166.4 2.3 %fusion.54 = f32[2,2,2,512,512]{4,3,2,1,0:T(8,128)} fusion(f32[2,2,2,512,512]{4,3,2,1,0:T(8,128)} %fusion.55, bf16[2,2,2,128,128]{4,3,2,1,0:T(8,128)(2,1)S(1)} %collective-permute-done.3, bf16[1,2,128,128]{3,2,1,0:T(8,128)(2,1)S(1)} %copy-done.1), kind=kOutput, calls=%fused_computation.56 | convolution fusion | flops 67371008 | bytes 1376256 | tf_op jit(solution)/shard_map/etpij,kj->etpik/dot_general | solution.py:45
  168.7 5.9 %fusion.49 = bf16[2,1,2,512,512]{4,3,2,1,0:T(8,128)(2,1)} fusion(f32[2,2,2,512,512]{4,3,2,1,0:T(8,128)} %fusion.54), kind=kLoop, calls=%fused_computation.47 | loop fusion | flops 3145728 | bytes 10485760 | tf_op jit(solution)/shard_map/convert_element_type | solution.py:87
  174.6 3.8 %slice.180 = bf16[2,1,2,512,512]{4,3,2,1,0:T(8,128)(2,1)} slice(f32[2,2,2,512,512]{4,3,2,1,0:T(8,128)} %fusion.54), slice={[0:2], [0:1], [0:2], [0:512], [0:512]} | slice | bytes 4194304 | tf_op jit(solution)/shard_map/slice | solution.py:85
  (1 shorter events, 0.0 us)
Async XLA Ops:
  0.6 18.5 %copy-start = (s32[4,3]{1,0:T(4,128)S(1)}, s32[4,3]{1,0:T(4,128)}, u32[]{:S(2)}) copy-start(s32[4,3]{1,0:T(4,128)} %param.23) | copy-start | bytes 148
  6.8 95.1 %collective-permute-start.1 = (bf16[2,2,2,512,512]{4,3,2,1,0:T(8,128)(2,1)}, bf16[2,2,2,512,512]{4,3,2,1,0:T(8,128)(2,1)}, u32[]{:S(2)}, u32[]{:S(2)}) collective-permute-start(bf16[2,2,2,512,512]{4,3,2,1,0:T(8,128)(2,1)} %constant_dynamic-update-slice_fusion), channel_id=1, source_target_pairs={{4,0},{8,4},{12,8},{16,12},{20,16},{24,20},{28,24},{32,28},{36,32}... | collective-permute-start | bytes 12582920 | tf_op jit(solution)/shard_map/ppermute | solution.py:23
  11.8 98.6 %collective-permute-start = (bf16[2,2,2,512,512]{4,3,2,1,0:T(8,128)(2,1)}, bf16[2,2,2,512,512]{4,3,2,1,0:T(8,128)(2,1)}, u32[]{:S(2)}, u32[]{:S(2)}) collective-permute-start(bf16[2,2,2,512,512]{4,3,2,1,0:T(8,128)(2,1)} %constant_dynamic-update-slice_fusion), channel_id=1, source_target_pairs={{0,4},{4,8},{8,12},{12,16},{16,20},{20,24},{24,28},{28,32},{32,36}... | collective-permute-start | bytes 12582920 | tf_op jit(solution)/shard_map/ppermute | solution.py:21
  14.8 151.6 %collective-permute-start.3 = (bf16[2,2,2,128,128]{4,3,2,1,0:T(8,128)(2,1)S(1)}, bf16[2,2,2,128,128]{4,3,2,1,0:T(8,128)(2,1)S(1)}, u32[]{:S(2)}, u32[]{:S(2)}) collective-permute-start(bf16[2,2,2,128,128]{4,3,2,1,0:T(8,128)(2,1)S(1)} %get-tuple-element.91), channel_id=1, source_target_pairs={{1,0},{2,1},{3,2},{5,4},{6,5},{7,6},{9,8},{10,9},{11,10},{13,12},{... | collective-permute-start | bytes 786440 | tf_op jit(solution)/shard_map/ppermute | solution.py:10
  16.7 147.4 %collective-permute-start.2 = (bf16[2,2,2,128,128]{4,3,2,1,0:T(8,128)(2,1)S(1)}, bf16[2,2,2,128,128]{4,3,2,1,0:T(8,128)(2,1)S(1)}, u32[]{:S(2)}, u32[]{:S(2)}) collective-permute-start(bf16[2,2,2,128,128]{4,3,2,1,0:T(8,128)(2,1)S(1)} %get-tuple-element.92), channel_id=1, source_target_pairs={{0,1},{1,2},{2,3},{4,5},{5,6},{6,7},{8,9},{9,10},{10,11},{12,13},{... | collective-permute-start | bytes 786440 | tf_op jit(solution)/shard_map/ppermute | solution.py:10
  21.8 99.0 %copy-start.2 = (f32[3]{0:T(128)S(1)}, f32[3]{0:T(128)}, u32[]{:S(2)}) copy-start(f32[3]{0:T(128)} %param.21) | copy-start | bytes 40
  21.8 99.0 %copy-start.3 = (bf16[1,3,512,512]{3,2,1,0:T(8,128)(2,1)S(1)}, bf16[1,3,512,512]{3,2,1,0:T(8,128)(2,1)}, u32[]{:S(2)}) copy-start(bf16[1,3,512,512]{3,2,1,0:T(8,128)(2,1)} %param.19) | copy-start | bytes 4718596
  21.8 99.0 %copy-start.4 = (s32[3]{0:T(128)S(1)}, s32[3]{0:T(128)}, u32[]{:S(2)}) copy-start(s32[3]{0:T(128)} %param.22) | copy-start | bytes 40
  148.4 15.7 %copy-start.1 = (bf16[1,2,128,128]{3,2,1,0:T(8,128)(2,1)S(1)}, bf16[1,2,128,128]{3,2,1,0:T(8,128)(2,1)}, u32[]{:S(2)}) copy-start(bf16[1,2,128,128]{3,2,1,0:T(8,128)(2,1)} %param.20) | copy-start | bytes 196612
where the time goes:
time: 179 us; the launch traced here: 178 us
  waiting for transfers between devices  88.5 us (49%)
  matrix products  37.3 us (21%)
  other arithmetic  18 us (10%)
  local copies, waits for them, and re-layouts  14.1 us (8%)
  starting transfers between devices  11.2 us (6%)
  loops' own time  6.7 us (4%)
  between operations  2.73 us (2%)
    ppermute x1, waiting for transfers between devices, extended(): lax.ppermute(head, axis, [((i + 1) % count, i) for i in range(ends)])  80 us
    dot_general x5, matrix products, sandwich(): jnp.einsum('etpij,kj->etpik', left_product, matrix, preferred_element_typ...  37.3 us
    concatenate x1, other arithmetic, extended(): jnp.concatenate([lax.ppermute(tail, axis, [(i, (i + 1) % count) for i in...  10.5 us
    ppermute x1, waiting for transfers between devices, extended(): lax.ppermute(tail, axis, [(i, (i + 1) % count) for i in range(ends)])  8.44 us
    another operation x3, loops' own time, body(): lax.cond(mode_flags[mode_index] > 0, add_mode, unchanged, accumulated)  6.7 us
    convert_element_type x1, other arithmetic, body(): retarded[:, None].astype(jnp.bfloat16)  5.9 us
    ppermute x1, starting transfers between devices, extended(): lax.ppermute(head, axis, [((i + 1) % count, i) for i in range(ends)])  4.92 us
    ppermute x2, starting transfers between devices, passed_along(): return lax.ppermute(x, axis, pairs)  4.34 us
  transfers between devices with their start and end apart: 4, of which 2 were waited for; matrix products, arithmetic and copies ran while one was open for 29% of the time, Pallas kernels for 0%

commit v1 on v0

v1 whole, which is shorter than its diff:
```python
import jax
import jax.numpy as jnp
from jax import lax
from jax.experimental import pallas as pl
from jax.experimental.pallas import tpu as pltpu
from jax.sharding import PartitionSpec as P


def shifted(x, energies, cuts, first):
    pairs = []
    for e in range(energies):
        for c in range(cuts):
            up = (c % 2 == 0) == first
            to = e + 1 if up else e - 1
            if 0 <= to < energies:
                pairs.append((e * cuts + c, to * cuts + c))
    return lax.ppermute(x, ("energy", "cuts"), pairs)


def passed_along(x, axis, by):
    length = lax.axis_size(axis)
    pairs = [(i, i + by) for i in range(length) if 0 <= i + by < length]
    return lax.ppermute(x, axis, pairs)


def product(a, b):
    return lax.dot_general(a, b, (((1,), (0,)), ((), ())), preferred_element_type=jnp.float32)


def product_t(a, b):
    return lax.dot_general(a, b, (((1,), (1,)), ((), ())), preferred_element_type=jnp.float32)


def far_kernel(slot, place, offsets, pattern, bose, lesser, greater, couple, low_out, ret_out, total):
    cut, core = place[0], place[1]
    energy = core if slot == 0 else 1 - core
    modes = couple.shape[1]
    total[...] = jnp.zeros_like(total)
    for mode in range(modes):

        @pl.when((pattern[cut, mode] > 0) & (offsets[mode] == 2))
        def _():
            matrix = couple[0, mode]
            for kind, green in enumerate((lesser, greater)):
                weight = bose[mode] + jnp.where(energy == kind, 0.0, 1.0)
                mixed = (green[0, 0, 0].astype(jnp.float32) * weight).astype(jnp.bfloat16)
                left = product(matrix, mixed).astype(jnp.bfloat16)
                total[kind] += product_t(left, matrix)

    low_out[0] = total[0].astype(jnp.bfloat16)
    ret_out[0] = (0.5 * (total[1] - total[0])).astype(jnp.bfloat16)


def far_terms(slot, scalars, bose, lesser, greater, couplings):
    orbitals = lesser.shape[-1]
    parts = lesser.shape[2]
    modes = couplings.shape[1]

    def green_at(p, place, *_):
        return (place[1] if slot == 0 else 1 - place[1], 0, p, 0, 0)

    green = pl.BlockSpec((1, 1, 1, orbitals, orbitals), green_at)
    out = pl.BlockSpec((1, orbitals, orbitals), lambda p, *_: (p, 0, 0))
    kernel = lambda *refs: far_kernel(slot, *refs)
    return pl.pallas_call(
        kernel,
        grid_spec=pltpu.PrefetchScalarGridSpec(
            num_scalar_prefetch=4,
            grid=(parts,),
            in_specs=[
                green,
                green,
                pl.BlockSpec((1, modes, orbitals, orbitals), lambda p, *_: (0, 0, 0, 0)),
            ],
            out_specs=[out, out],
            scratch_shapes=[pltpu.VMEM((2, orbitals, orbitals), jnp.float32)],
        ),
        out_shape=[jax.ShapeDtypeStruct((parts, orbitals, orbitals), jnp.bfloat16)] * 2,
        compiler_params=pltpu.CompilerParams(vmem_limit_bytes=40 * 2**20),
        cost_estimate=pl.CostEstimate(
            flops=parts * 2 * modes * 4 * orbitals**3, bytes_accessed=6 * 2**20, transcendentals=0
        ),
        name="far_terms",
    )(*scalars, bose, lesser, greater, couplings)


def near_kernel(
    place, offsets, pattern, bose,
    lesser, greater, first_low, first_high, second_low, second_high,
    corner_low, corner_high, couple, rim, low_out, ret_out, total,
):
    cut, core = place[0], place[1]
    slot = pl.program_id(1)
    energy = jnp.where(slot == 0, core, 1 - core)
    modes = couple.shape[1]
    orbitals = couple.shape[-1]
    width = rim.shape[-1]
    greens = (lesser, greater)
    first = (first_low, first_high)
    second = (second_low, second_high)
    total[...] = jnp.zeros_like(total)
    for mode in range(modes):
        here = pattern[cut, mode] > 0
        wide = offsets[mode] == 2

        @pl.when(here)
        def _():
            matrix = couple[0, mode]
            for kind in range(2):
                same = bose[mode] + jnp.where(energy == kind, 1.0, 0.0)
                other = bose[mode] + jnp.where(energy == kind, 0.0, 1.0)
                own = jnp.where(wide, 0.0, same)
                cross = jnp.where(wide, same, other)
                use_first = wide == (slot == 1)
                a = jnp.where(use_first, cross, 0.0)
                b = jnp.where(use_first, 0.0, cross)
                mixed = (
                    greens[kind][0, 0, 0].astype(jnp.float32) * own
                    + first[kind][0, 0, 0].astype(jnp.float32) * a
                    + second[kind][0, 0, 0].astype(jnp.float32) * b
                ).astype(jnp.bfloat16)
                left = product(matrix, mixed).astype(jnp.bfloat16)
                total[kind] += product_t(left, matrix)

    for kind in range(2):
        for side, corner in enumerate((corner_low, corner_high)):
            matrix = rim[0, side]
            left = product(matrix, corner[0, kind, 0]).astype(jnp.bfloat16)
            at = slice(0, width) if side == 0 else slice(orbitals - width, orbitals)
            total[kind, at, at] += product_t(left, matrix)
    low_out[0, 0] = total[0]
    ret_out[0, 0] = 0.5 * (total[1] - total[0])


def near_terms(scalars, bose, lesser, greater, near, corners, couplings, rim_couple):
    orbitals = lesser.shape[-1]
    parts = lesser.shape[2]
    modes = couplings.shape[1]
    width = rim_couple.shape[-1]

    def energy_of(j, place):
        return jnp.where(j == 0, place[1], 1 - place[1])

    own = pl.BlockSpec(
        (1, 1, 1, orbitals, orbitals), lambda p, j, place, *_: (1 - energy_of(j, place), 0, p, 0, 0)
    )
    arrived = pl.BlockSpec((1, 1, 1, orbitals, orbitals), lambda p, j, *_: (0, 0, p, 0, 0))
    corner = pl.BlockSpec(
        (1, 2, 1, width, width), lambda p, j, place, *_: (energy_of(j, place), 0, p, 0, 0)
    )
    out = pl.BlockSpec((1, 1, orbitals, orbitals), lambda p, j, *_: (j, p, 0, 0))
    return pl.pallas_call(
        near_kernel,
        grid_spec=pltpu.PrefetchScalarGridSpec(
            num_scalar_prefetch=4,
            grid=(parts, 2),
            in_specs=[own, own, arrived, arrived, arrived, arrived, corner, corner]
            + [
                pl.BlockSpec((1, modes, orbitals, orbitals), lambda p, j, *_: (0, 0, 0, 0)),
                pl.BlockSpec((1, 2, width, width), lambda p, j, *_: (0, 0, 0, 0)),
            ],
            out_specs=[out, out],
            scratch_shapes=[pltpu.VMEM((2, orbitals, orbitals), jnp.float32)],
        ),
        out_shape=[jax.ShapeDtypeStruct((2, parts, orbitals, orbitals), jnp.float32)] * 2,
        compiler_params=pltpu.CompilerParams(vmem_limit_bytes=40 * 2**20),
        cost_estimate=pl.CostEstimate(
            flops=parts * 4 * modes * 4 * orbitals**3, bytes_accessed=20 * 2**20, transcendentals=0
        ),
        name="near_terms",
    )(*scalars, bose, lesser, greater, *near, *corners, couplings, rim_couple)


def add_kernel(place, near, far_first, far_second, out):
    core = place[1]
    out[core, 0, 0] = (near[0, 0] + far_first[0].astype(jnp.float32)).astype(out.dtype)
    out[1 - core, 0, 0] = (near[1, 0] + far_second[0].astype(jnp.float32)).astype(out.dtype)


def added(place, near, far_first, far_second):
    parts, orbitals = near.shape[1], near.shape[-1]
    rows = orbitals // 2
    far = pl.BlockSpec((1, rows, orbitals), lambda p, r, *_: (p, r, 0))
    return pl.pallas_call(
        add_kernel,
        grid_spec=pltpu.PrefetchScalarGridSpec(
            num_scalar_prefetch=1,
            grid=(parts, orbitals // rows),
            in_specs=[
                pl.BlockSpec((2, 1, rows, orbitals), lambda p, r, *_: (0, p, r, 0)),
                far,
                far,
            ],
            out_specs=pl.BlockSpec((2, 1, 1, rows, orbitals), lambda p, r, *_: (0, 0, p, r, 0)),
        ),
        out_shape=jax.ShapeDtypeStruct((2, 1, parts, orbitals, orbitals), jnp.bfloat16),
        compiler_params=pltpu.CompilerParams(vmem_limit_bytes=24 * 2**20),
        cost_estimate=pl.CostEstimate(
            flops=4 * orbitals**2, bytes_accessed=8 * 2**20, transcendentals=0
        ),
        name="added",
    )(place, near, far_first, far_second)


def body(lesser, greater, couplings, rim_couple, bose_factor, offsets, pattern):
    energies = lax.axis_size("energy")
    cuts = lax.axis_size("cuts")
    orbitals = lesser.shape[-1]
    rim_width = rim_couple.shape[-1]
    cut = lax.axis_index("cuts")
    core = cut % 2
    place = jnp.stack([cut, core]).astype(jnp.int32)
    scalars = (place, offsets, pattern)

    near = []
    for first in (True, False):
        for green in (lesser, greater):
            sent = lax.dynamic_slice_in_dim(green, 1 - core if first else core, 1, 0)
            near.append(shifted(sent, energies, cuts, first))

    corners = []
    for by in (1, -1):
        edge = slice(orbitals - rim_width, orbitals) if by == 1 else slice(0, rim_width)
        sent = jnp.concatenate([lesser[..., edge, edge], greater[..., edge, edge]], 1)
        corners.append(passed_along(sent, "cuts", by))

    far_low, far_ret = [], []
    for slot in range(2):
        low, ret = far_terms(slot, scalars, bose_factor, lesser, greater, couplings)
        far_low.append(shifted(low, energies, cuts, slot == 0))
        far_ret.append(shifted(ret, energies, cuts, slot == 0))

    low, ret = near_terms(
        scalars, bose_factor, lesser, greater, near, corners, couplings, rim_couple
    )
    return added(place, low, *far_low), added(place, ret, *far_ret)


def solution(mesh):
    return jax.shard_map(
        body,
        mesh=mesh,
        in_specs=(
            P("energy", "cuts", None, None, None),
            P("energy", "cuts", None, None, None),
            P("cuts", None, None, None),
            P("cuts", None, None, None),
            P(),
            P(),
            P(),
        ),
        out_specs=(P("energy", "cuts", None, None, None), P("energy", "cuts", None, None, None)),
        check_vma=False,
    )
```

time: 179 us -> 123 us (0.69)
  the two profiles are of different devices: /device:TPU:144 before, /device:TPU:110 now
where the time goes in v1:
time: 123 us; the launch traced here: 121 us
  waiting for transfers between devices  55.7 us (45%)
  starting transfers between devices  41.6 us (34%)
  Pallas kernels  18.5 us (15%)
  local copies, waits for them, and re-layouts  4.3 us (3%)
    ppermute x8, starting transfers between devices, shifted(): return lax.ppermute(x, ('energy', 'cuts'), pairs)  36.3 us
    ppermute x2, waiting for transfers between devices, passed_along(): return lax.ppermute(x, axis, pairs)  29.8 us
    ppermute x8, waiting for transfers between devices, shifted(): return lax.ppermute(x, ('energy', 'cuts'), pairs)  25.8 us
    pallas_call x1, Pallas kernels, near_terms(): pl.pallas_call(near_kernel, grid_spec=pltpu.PrefetchScalarGridSpec(num_sc...  10.6 us
    pallas_call x2, Pallas kernels, added(): pl.pallas_call(add_kernel, grid_spec=pltpu.PrefetchScalarGridSpec(num_sca...  5.47 us
    ppermute x2, starting transfers between devices, passed_along(): return lax.ppermute(x, axis, pairs)  5.23 us
  transfers between devices with their start and end apart: 10, of which 4 were waited for; matrix products, arithmetic and copies ran while one was open for 0% of the time, Pallas kernels for 13%

profile of v1, /device:TPU:110, one launch (start us, length us, event | category | flops | bytes accessed | tf_op | source)
XLA Modules:
  0.0 121.1 jit_solution(3922105227062601911)
XLA Ops:
  0.7 0.0 copy-start.2
  0.7 1.8 %constant_dynamic-slice_fusion = (bf16[1,1,2,512,512]{4,3,2,1,0:T(8,128)(2,1)S(1)}, bf16[1,1,2,512,512]{4,3,2,1,0:T(8,128)(2,1)S(1)}) fusion(bf16[2,1,2,512,512]{4,3,2,1,0:T(8,128)(2,1)} %refs_5_.3, s32[]{:T(128)S(6)} %select_n.17, s32[]{:T(128)S(6)} %select_n.16), kind=kLoop, calls=%fused_computation.2 | loop fusion | bytes 4194312 | tf_op jit(solution)/shard_map/dynamic_slice | solution.py:218
  2.5 4.8 %collective-permute-start.1 = (bf16[1,1,2,512,512]{4,3,2,1,0:T(8,128)(2,1)S(1)}, bf16[1,1,2,512,512]{4,3,2,1,0:T(8,128)(2,1)S(1)}, u32[]{:S(2)}, u32[]{:S(2)}) collective-permute-start(bf16[1,1,2,512,512]{4,3,2,1,0:T(8,128)(2,1)S(1)} %get-tuple-element.19), channel_id=1, source_target_pairs={{0,4},{2,6},{4,8},{5,1},{6,10},{7,3},{8,12},{9,5},{10,14},{11,7},{... | collective-permute-start | bytes 3145736 | tf_op jit(solution)/shard_map/ppermute | solution.py:17
  7.3 0.0 copy-start.3
  7.3 0.0 copy-start.4
  7.4 0.0 copy-start.6
  7.4 0.0 copy-start.7
  7.4 0.0 copy-start.8
  7.4 2.2 %collective-permute-start.3 = (bf16[1,1,2,512,512]{4,3,2,1,0:T(8,128)(2,1)S(1)}, bf16[1,1,2,512,512]{4,3,2,1,0:T(8,128)(2,1)S(1)}, u32[]{:S(2)}, u32[]{:S(2)}) collective-permute-start(bf16[1,1,2,512,512]{4,3,2,1,0:T(8,128)(2,1)S(1)} %get-tuple-element.18), channel_id=1, source_target_pairs={{1,5},{3,7},{4,0},{5,9},{6,2},{7,11},{8,4},{9,13},{10,6},{11,15},{... | collective-permute-start | bytes 3145736 | tf_op jit(solution)/shard_map/ppermute | solution.py:17
  9.6 0.0 copy-done.2
  9.6 0.1 constant_dynamic-slice_fusion.1
  9.8 8.1 %collective-permute-start = (bf16[1,1,2,512,512]{4,3,2,1,0:T(8,128)(2,1)S(1)}, bf16[1,1,2,512,512]{4,3,2,1,0:T(8,128)(2,1)S(1)}, u32[]{:S(2)}, u32[]{:S(2)}) collective-permute-start(bf16[1,1,2,512,512]{4,3,2,1,0:T(8,128)(2,1)S(1)} %get-tuple-element.21), channel_id=1, source_target_pairs={{0,4},{2,6},{4,8},{5,1},{6,10},{7,3},{8,12},{9,5},{10,14},{11,7},{... | collective-permute-start | bytes 3145736 | tf_op jit(solution)/shard_map/ppermute | solution.py:17
  17.9 1.9 %collective-permute-start.2 = (bf16[1,1,2,512,512]{4,3,2,1,0:T(8,128)(2,1)S(1)}, bf16[1,1,2,512,512]{4,3,2,1,0:T(8,128)(2,1)S(1)}, u32[]{:S(2)}, u32[]{:S(2)}) collective-permute-start(bf16[1,1,2,512,512]{4,3,2,1,0:T(8,128)(2,1)S(1)} %get-tuple-element.20), channel_id=1, source_target_pairs={{1,5},{3,7},{4,0},{5,9},{6,2},{7,11},{8,4},{9,13},{10,6},{11,15},{... | collective-permute-start | bytes 3145736 | tf_op jit(solution)/shard_map/ppermute | solution.py:17
  19.9 0.0 copy-done.3
  20.0 3.9 %collective-permute-start.4 = (bf16[2,2,2,128,128]{4,3,2,1,0:T(8,128)(2,1)S(1)}, bf16[2,2,2,128,128]{4,3,2,1,0:T(8,128)(2,1)S(1)}, u32[]{:S(2)}, u32[]{:S(2)}) collective-permute-start(bf16[2,2,2,128,128]{4,3,2,1,0:T(8,128)(2,1)S(1)} %pad_maximum_fusion), channel_id=1, source_target_pairs={{0,1},{1,2},{2,3},{4,5},{5,6},{6,7},{8,9},{9,10},{10,11},{12,13},{... | collective-permute-start | bytes 786440 | tf_op jit(solution)/shard_map/ppermute | solution.py:23
  23.9 0.1 pad_add_fusion.place.refs_0_
  24.0 0.0 copy-done.4
  24.0 0.0 copy-done.6
  24.0 0.0 copy-done.7
  24.0 0.0 copy-done.8
  24.0 1.2 %far_terms.2 = (bf16[2,512,512]{2,1,0:T(8,128)(2,1)S(1)}, bf16[2,512,512]{2,1,0:T(8,128)(2,1)S(1)}) custom-call(s32[2]{0:T(128)S(1)} %pad_add_fusion.place.refs_0_, s32[3]{0:T(128)S(1)} %copy-done.7, s32[4,3]{1,0:T(4,128)S(1)} %copy-done.6, f32[3]{0:T(128)S(1)} %copy-done.8, bf16[2,1,2,512,512]{4,3,2,1,0:T(8,128)(2,1)S(1)} %copy-done.2, ...), custom_call_target="tpu_custom_call" | custom-call | flops 6442450944 | bytes 6291456 | tf_op jit(solution)/shard_map/far_terms/pallas_call | solution.py:65
  25.3 0.0 copy-start.5
  25.3 0.0 collective-permute-done.4.corner_low
  25.3 1.3 %collective-permute-start.5 = (bf16[2,2,2,128,128]{4,3,2,1,0:T(8,128)(2,1)S(1)}, bf16[2,2,2,128,128]{4,3,2,1,0:T(8,128)(2,1)S(1)}, u32[]{:S(2)}, u32[]{:S(2)}) collective-permute-start(bf16[2,2,2,128,128]{4,3,2,1,0:T(8,128)(2,1)S(1)} %pad_maximum_fusion.1), channel_id=1, source_target_pairs={{1,0},{2,1},{3,2},{5,4},{6,5},{7,6},{9,8},{10,9},{11,10},{13,12},{... | collective-permute-start | bytes 786440 | tf_op jit(solution)/shard_map/ppermute | solution.py:23
  26.6 1.2 %far_terms.3 = (bf16[2,512,512]{2,1,0:T(8,128)(2,1)S(1)}, bf16[2,512,512]{2,1,0:T(8,128)(2,1)S(1)}) custom-call(s32[2]{0:T(128)S(1)} %pad_add_fusion.place.refs_0_, s32[3]{0:T(128)S(1)} %copy-done.7, s32[4,3]{1,0:T(4,128)S(1)} %copy-done.6, f32[3]{0:T(128)S(1)} %copy-done.8, bf16[2,1,2,512,512]{4,3,2,1,0:T(8,128)(2,1)S(1)} %copy-done.2, ...), custom_call_target="tpu_custom_call" | custom-call | flops 6442450944 | bytes 6291456 | tf_op jit(solution)/shard_map/far_terms/pallas_call | solution.py:65
  27.8 29.8 %collective-permute-done.5.corner_high = bf16[2,2,2,128,128]{4,3,2,1,0:T(8,128)(2,1)S(1)} collective-permute-done((bf16[2,2,2,128,128]{4,3,2,1,0:T(8,128)(2,1)S(1)}, bf16[2,2,2,128,128]{4,3,2,1,0:T(8,128)(2,1)S(1)}, u32[]{:S(2)}, u32[]{:S(2)}) %collective-permute-start.5) | collective-permute-done | bytes 262176 | tf_op jit(solution)/shard_map/ppermute | solution.py:23
  57.7 7.1 %collective-permute-start.8 = (bf16[2,512,512]{2,1,0:T(8,128)(2,1)S(1)}, bf16[2,512,512]{2,1,0:T(8,128)(2,1)S(1)}, u32[]{:S(2)}, u32[]{:S(2)}) collective-permute-start(bf16[2,512,512]{2,1,0:T(8,128)(2,1)S(1)} %get-tuple-element.12), channel_id=1, source_target_pairs={{0,4},{2,6},{4,8},{5,1},{6,10},{7,3},{8,12},{9,5},{10,14},{11,7},{... | collective-permute-start | bytes 3145736 | tf_op jit(solution)/shard_map/ppermute | solution.py:17
  64.8 0.0 collective-permute-done.1.first_high
  64.8 1.9 %collective-permute-start.9 = (bf16[2,512,512]{2,1,0:T(8,128)(2,1)S(1)}, bf16[2,512,512]{2,1,0:T(8,128)(2,1)S(1)}, u32[]{:S(2)}, u32[]{:S(2)}) collective-permute-start(bf16[2,512,512]{2,1,0:T(8,128)(2,1)S(1)} %get-tuple-element.13), channel_id=1, source_target_pairs={{1,5},{3,7},{4,0},{5,9},{6,2},{7,11},{8,4},{9,13},{10,6},{11,15},{... | collective-permute-start | bytes 3145736 | tf_op jit(solution)/shard_map/ppermute | solution.py:17
  66.7 0.0 collective-permute-done.3.second_high
  66.7 8.1 %collective-permute-start.6 = (bf16[2,512,512]{2,1,0:T(8,128)(2,1)S(1)}, bf16[2,512,512]{2,1,0:T(8,128)(2,1)S(1)}, u32[]{:S(2)}, u32[]{:S(2)}) collective-permute-start(bf16[2,512,512]{2,1,0:T(8,128)(2,1)S(1)} %get-tuple-element.9), channel_id=1, source_target_pairs={{0,4},{2,6},{4,8},{5,1},{6,10},{7,3},{8,12},{9,5},{10,14},{11,7},{... | collective-permute-start | bytes 3145736 | tf_op jit(solution)/shard_map/ppermute | solution.py:17
  74.9 0.0 collective-permute-done.first_low
  74.9 2.1 %collective-permute-start.7 = (bf16[2,512,512]{2,1,0:T(8,128)(2,1)S(1)}, bf16[2,512,512]{2,1,0:T(8,128)(2,1)S(1)}, u32[]{:S(2)}, u32[]{:S(2)}) collective-permute-start(bf16[2,512,512]{2,1,0:T(8,128)(2,1)S(1)} %get-tuple-element.10), channel_id=1, source_target_pairs={{1,5},{3,7},{4,0},{5,9},{6,2},{7,11},{8,4},{9,13},{10,6},{11,15},{... | collective-permute-start | bytes 3145736 | tf_op jit(solution)/shard_map/ppermute | solution.py:17
  77.0 0.0 collective-permute-done.2.second_low
  77.0 0.0 copy-done.5
  77.0 10.6 %near_terms.1 = (f32[2,2,512,512]{3,2,1,0:T(8,128)}, f32[2,2,512,512]{3,2,1,0:T(8,128)}) custom-call(s32[2]{0:T(128)S(1)} %pad_add_fusion.place.refs_0_, s32[3]{0:T(128)S(1)} %copy-done.7, s32[4,3]{1,0:T(4,128)S(1)} %copy-done.6, f32[3]{0:T(128)S(1)} %copy-done.8, bf16[2,1,2,512,512]{4,3,2,1,0:T(8,128)(2,1)S(1)} %copy-done.2, ...), custom_call_target="tpu_custom_call" | custom-call | flops 12884901888 | bytes 20971520 | tf_op jit(solution)/shard_map/near_terms/pallas_call | solution.py:152
  87.6 0.0 collective-permute-done.8.far_first
  87.6 9.3 %collective-permute-done.9.far_second = bf16[2,512,512]{2,1,0:T(8,128)(2,1)S(1)} collective-permute-done((bf16[2,512,512]{2,1,0:T(8,128)(2,1)S(1)}, bf16[2,512,512]{2,1,0:T(8,128)(2,1)S(1)}, u32[]{:S(2)}, u32[]{:S(2)}) %collective-permute-start.9) | collective-permute-done | bytes 1048608 | tf_op jit(solution)/shard_map/ppermute | solution.py:17
  96.9 0.0 copy-start.1
  96.9 2.2 %copy-done.1 = f32[2,2,512,512]{3,2,1,0:T(8,128)S(1)} copy-done((f32[2,2,512,512]{3,2,1,0:T(8,128)S(1)}, f32[2,2,512,512]{3,2,1,0:T(8,128)}, u32[]{:S(2)}) %copy-start.1) | copy-done | bytes 4194328
  99.1 0.0 copy-start
  99.1 2.7 %added.3 = bf16[2,1,2,512,512]{4,3,2,1,0:T(8,128)(2,1)} custom-call(s32[2]{0:T(128)S(1)} %pad_add_fusion.place.refs_0_, f32[2,2,512,512]{3,2,1,0:T(8,128)S(1)} %copy-done.1, bf16[2,512,512]{2,1,0:T(8,128)(2,1)S(1)} %collective-permute-done.8.far_first, bf16[2,512,512]{2,1,0:T(8,128)(2,1)S(1)} %collective-permute-done.9.far_second), custom_call_target="tpu_custom_call" | custom-call | flops 1048576 | bytes 8388608 | tf_op jit(solution)/shard_map/added/pallas_call | solution.py:184
  101.9 0.1 collective-permute-done.6.far_first
  102.0 16.4 %collective-permute-done.7.far_second = bf16[2,512,512]{2,1,0:T(8,128)(2,1)S(1)} collective-permute-done((bf16[2,512,512]{2,1,0:T(8,128)(2,1)S(1)}, bf16[2,512,512]{2,1,0:T(8,128)(2,1)S(1)}, u32[]{:S(2)}, u32[]{:S(2)}) %collective-permute-start.7) | collective-permute-done | bytes 1048608 | tf_op jit(solution)/shard_map/ppermute | solution.py:17
  118.3 0.0 copy-done
  118.3 2.7 %added.2 = bf16[2,1,2,512,512]{4,3,2,1,0:T(8,128)(2,1)} custom-call(s32[2]{0:T(128)S(1)} %pad_add_fusion.place.refs_0_, f32[2,2,512,512]{3,2,1,0:T(8,128)S(1)} %copy-done, bf16[2,512,512]{2,1,0:T(8,128)(2,1)S(1)} %collective-permute-done.6.far_first, bf16[2,512,512]{2,1,0:T(8,128)(2,1)S(1)} %collective-permute-done.7.far_second), custom_call_target="tpu_custom_call" | custom-call | flops 1048576 | bytes 8388608 | tf_op jit(solution)/shard_map/added/pallas_call | solution.py:184
  (4 shorter events, 0.2 us)
Async XLA Ops:
  0.7 8.9 %copy-start.2 = (bf16[2,1,2,512,512]{4,3,2,1,0:T(8,128)(2,1)S(1)}, bf16[2,1,2,512,512]{4,3,2,1,0:T(8,128)(2,1)}, u32[]{:S(2)}) copy-start(bf16[2,1,2,512,512]{4,3,2,1,0:T(8,128)(2,1)} %refs_4_.3) | copy-start | bytes 6291460
  2.5 62.3 %collective-permute-start.1 = (bf16[1,1,2,512,512]{4,3,2,1,0:T(8,128)(2,1)S(1)}, bf16[1,1,2,512,512]{4,3,2,1,0:T(8,128)(2,1)S(1)}, u32[]{:S(2)}, u32[]{:S(2)}) collective-permute-start(bf16[1,1,2,512,512]{4,3,2,1,0:T(8,128)(2,1)S(1)} %get-tuple-element.19), channel_id=1, source_target_pairs={{0,4},{2,6},{4,8},{5,1},{6,10},{7,3},{8,12},{9,5},{10,14},{11,7},{... | collective-permute-start | bytes 3145736 | tf_op jit(solution)/shard_map/ppermute | solution.py:17
  7.3 12.5 %copy-start.3 = (bf16[2,1,2,512,512]{4,3,2,1,0:T(8,128)(2,1)S(1)}, bf16[2,1,2,512,512]{4,3,2,1,0:T(8,128)(2,1)}, u32[]{:S(2)}) copy-start(bf16[2,1,2,512,512]{4,3,2,1,0:T(8,128)(2,1)} %refs_5_.3) | copy-start | bytes 6291460
  7.3 16.7 %copy-start.4 = (bf16[1,3,512,512]{3,2,1,0:T(8,128)(2,1)S(1)}, bf16[1,3,512,512]{3,2,1,0:T(8,128)(2,1)}, u32[]{:S(2)}) copy-start(bf16[1,3,512,512]{3,2,1,0:T(8,128)(2,1)} %refs_6_.3) | copy-start | bytes 4718596
  7.4 16.7 %copy-start.6 = (s32[4,3]{1,0:T(4,128)S(1)}, s32[4,3]{1,0:T(4,128)}, u32[]{:S(2)}) copy-start(s32[4,3]{1,0:T(4,128)} %refs_2_.3) | copy-start | bytes 148
  7.4 16.6 %copy-start.7 = (s32[3]{0:T(128)S(1)}, s32[3]{0:T(128)}, u32[]{:S(2)}) copy-start(s32[3]{0:T(128)} %refs_1_.3) | copy-start | bytes 40
  7.4 16.6 %copy-start.8 = (f32[3]{0:T(128)S(1)}, f32[3]{0:T(128)}, u32[]{:S(2)}) copy-start(f32[3]{0:T(128)} %refs_3_.3) | copy-start | bytes 40
  7.4 59.3 %collective-permute-start.3 = (bf16[1,1,2,512,512]{4,3,2,1,0:T(8,128)(2,1)S(1)}, bf16[1,1,2,512,512]{4,3,2,1,0:T(8,128)(2,1)S(1)}, u32[]{:S(2)}, u32[]{:S(2)}) collective-permute-start(bf16[1,1,2,512,512]{4,3,2,1,0:T(8,128)(2,1)S(1)} %get-tuple-element.18), channel_id=1, source_target_pairs={{1,5},{3,7},{4,0},{5,9},{6,2},{7,11},{8,4},{9,13},{10,6},{11,15},{... | collective-permute-start | bytes 3145736 | tf_op jit(solution)/shard_map/ppermute | solution.py:17
  9.8 65.1 %collective-permute-start = (bf16[1,1,2,512,512]{4,3,2,1,0:T(8,128)(2,1)S(1)}, bf16[1,1,2,512,512]{4,3,2,1,0:T(8,128)(2,1)S(1)}, u32[]{:S(2)}, u32[]{:S(2)}) collective-permute-start(bf16[1,1,2,512,512]{4,3,2,1,0:T(8,128)(2,1)S(1)} %get-tuple-element.21), channel_id=1, source_target_pairs={{0,4},{2,6},{4,8},{5,1},{6,10},{7,3},{8,12},{9,5},{10,14},{11,7},{... | collective-permute-start | bytes 3145736 | tf_op jit(solution)/shard_map/ppermute | solution.py:17
  17.9 59.1 %collective-permute-start.2 = (bf16[1,1,2,512,512]{4,3,2,1,0:T(8,128)(2,1)S(1)}, bf16[1,1,2,512,512]{4,3,2,1,0:T(8,128)(2,1)S(1)}, u32[]{:S(2)}, u32[]{:S(2)}) collective-permute-start(bf16[1,1,2,512,512]{4,3,2,1,0:T(8,128)(2,1)S(1)} %get-tuple-element.20), channel_id=1, source_target_pairs={{1,5},{3,7},{4,0},{5,9},{6,2},{7,11},{8,4},{9,13},{10,6},{11,15},{... | collective-permute-start | bytes 3145736 | tf_op jit(solution)/shard_map/ppermute | solution.py:17
  20.0 5.3 %collective-permute-start.4 = (bf16[2,2,2,128,128]{4,3,2,1,0:T(8,128)(2,1)S(1)}, bf16[2,2,2,128,128]{4,3,2,1,0:T(8,128)(2,1)S(1)}, u32[]{:S(2)}, u32[]{:S(2)}) collective-permute-start(bf16[2,2,2,128,128]{4,3,2,1,0:T(8,128)(2,1)S(1)} %pad_maximum_fusion), channel_id=1, source_target_pairs={{0,1},{1,2},{2,3},{4,5},{5,6},{6,7},{8,9},{9,10},{10,11},{12,13},{... | collective-permute-start | bytes 786440 | tf_op jit(solution)/shard_map/ppermute | solution.py:23
  25.3 51.7 %copy-start.5 = (bf16[1,2,128,128]{3,2,1,0:T(8,128)(2,1)S(1)}, bf16[1,2,128,128]{3,2,1,0:T(8,128)(2,1)}, u32[]{:S(2)}) copy-start(bf16[1,2,128,128]{3,2,1,0:T(8,128)(2,1)} %rim.1) | copy-start | bytes 196612
  25.3 32.4 %collective-permute-start.5 = (bf16[2,2,2,128,128]{4,3,2,1,0:T(8,128)(2,1)S(1)}, bf16[2,2,2,128,128]{4,3,2,1,0:T(8,128)(2,1)S(1)}, u32[]{:S(2)}, u32[]{:S(2)}) collective-permute-start(bf16[2,2,2,128,128]{4,3,2,1,0:T(8,128)(2,1)S(1)} %pad_maximum_fusion.1), channel_id=1, source_target_pairs={{1,0},{2,1},{3,2},{5,4},{6,5},{7,6},{9,8},{10,9},{11,10},{13,12},{... | collective-permute-start | bytes 786440 | tf_op jit(solution)/shard_map/ppermute | solution.py:23
  57.7 29.9 %collective-permute-start.8 = (bf16[2,512,512]{2,1,0:T(8,128)(2,1)S(1)}, bf16[2,512,512]{2,1,0:T(8,128)(2,1)S(1)}, u32[]{:S(2)}, u32[]{:S(2)}) collective-permute-start(bf16[2,512,512]{2,1,0:T(8,128)(2,1)S(1)} %get-tuple-element.12), channel_id=1, source_target_pairs={{0,4},{2,6},{4,8},{5,1},{6,10},{7,3},{8,12},{9,5},{10,14},{11,7},{... | collective-permute-start | bytes 3145736 | tf_op jit(solution)/shard_map/ppermute | solution.py:17
  64.8 32.2 %collective-permute-start.9 = (bf16[2,512,512]{2,1,0:T(8,128)(2,1)S(1)}, bf16[2,512,512]{2,1,0:T(8,128)(2,1)S(1)}, u32[]{:S(2)}, u32[]{:S(2)}) collective-permute-start(bf16[2,512,512]{2,1,0:T(8,128)(2,1)S(1)} %get-tuple-element.13), channel_id=1, source_target_pairs={{1,5},{3,7},{4,0},{5,9},{6,2},{7,11},{8,4},{9,13},{10,6},{11,15},{... | collective-permute-start | bytes 3145736 | tf_op jit(solution)/shard_map/ppermute | solution.py:17
  66.7 35.2 %collective-permute-start.6 = (bf16[2,512,512]{2,1,0:T(8,128)(2,1)S(1)}, bf16[2,512,512]{2,1,0:T(8,128)(2,1)S(1)}, u32[]{:S(2)}, u32[]{:S(2)}) collective-permute-start(bf16[2,512,512]{2,1,0:T(8,128)(2,1)S(1)} %get-tuple-element.9), channel_id=1, source_target_pairs={{0,4},{2,6},{4,8},{5,1},{6,10},{7,3},{8,12},{9,5},{10,14},{11,7},{... | collective-permute-start | bytes 3145736 | tf_op jit(solution)/shard_map/ppermute | solution.py:17
  74.9 43.4 %collective-permute-start.7 = (bf16[2,512,512]{2,1,0:T(8,128)(2,1)S(1)}, bf16[2,512,512]{2,1,0:T(8,128)(2,1)S(1)}, u32[]{:S(2)}, u32[]{:S(2)}) collective-permute-start(bf16[2,512,512]{2,1,0:T(8,128)(2,1)S(1)} %get-tuple-element.10), channel_id=1, source_target_pairs={{1,5},{3,7},{4,0},{5,9},{6,2},{7,11},{8,4},{9,13},{10,6},{11,15},{... | collective-permute-start | bytes 3145736 | tf_op jit(solution)/shard_map/ppermute | solution.py:17
  96.9 2.2 %copy-start.1 = (f32[2,2,512,512]{3,2,1,0:T(8,128)S(1)}, f32[2,2,512,512]{3,2,1,0:T(8,128)}, u32[]{:S(2)}) copy-start(f32[2,2,512,512]{3,2,1,0:T(8,128)} %get-tuple-element.11.near) | copy-start | bytes 12582916
  99.1 19.2 %copy-start = (f32[2,2,512,512]{3,2,1,0:T(8,128)S(1)}, f32[2,2,512,512]{3,2,1,0:T(8,128)}, u32[]{:S(2)}) copy-start(f32[2,2,512,512]{3,2,1,0:T(8,128)} %get-tuple-element.8.near) | copy-start | bytes 12582916

commit v2 on v1

v2 whole, which is shorter than its diff:
```python
import functools

import jax
import jax.numpy as jnp
from jax import lax
from jax.experimental import pallas as pl
from jax.experimental.pallas import tpu as pltpu
from jax.sharding import PartitionSpec as P


def swapped(x, energies, cuts, inside):
    pairs = []
    for e in range(energies):
        for c in range(cuts):
            to = c ^ 1 if inside else (c + 1 if c % 2 else c - 1)
            if 0 <= to < cuts:
                pairs.append((e * cuts + c, e * cuts + to))
    return lax.ppermute(x, ("energy", "cuts"), pairs)


def shifted(x, energies, cuts, first):
    pairs = []
    for e in range(energies):
        for c in range(cuts):
            up = (c % 2 == 0) == first
            to = e + 1 if up else e - 1
            if 0 <= to < energies:
                pairs.append((e * cuts + c, to * cuts + c))
    return lax.ppermute(x, ("energy", "cuts"), pairs)


def product(a, b):
    return lax.dot_general(a, b, (((1,), (0,)), ((), ())), preferred_element_type=jnp.float32)


def product_t(a, b):
    return lax.dot_general(a, b, (((1,), (1,)), ((), ())), preferred_element_type=jnp.float32)


def run_copies(pairs, sems):
    copies = [pltpu.make_async_copy(src, dst, sems.at[i]) for i, (src, dst) in enumerate(pairs)]
    for copy in copies:
        copy.start()
    for copy in copies:
        copy.wait()


def corner_kernel(width, place, lesser, greater, inner, outer, sems):
    core = place[1]
    span = lesser.shape[-1] - width
    pairs = []
    for kind, green in enumerate((lesser, greater)):
        for far_side, out in ((core, outer), (1 - core, inner)):
            edge = pl.ds(pl.multiple_of(far_side * span, width), width)
            pairs.append((green.at[:, 0, :, edge, edge], out.at[:, kind]))
    run_copies(pairs, sems)


def near_copy_kernel(first, place, lesser, greater, near, sems):
    at = 1 - place[1] if first else place[1]
    greens = enumerate((lesser, greater))
    run_copies([(green.at[at, 0], near.at[kind]) for kind, green in greens], sems)


def copied(kernel, shapes, copies, place, lesser, greater):
    anywhere = pl.BlockSpec(memory_space=pl.ANY)
    return pl.pallas_call(
        kernel,
        grid_spec=pltpu.PrefetchScalarGridSpec(
            num_scalar_prefetch=1,
            grid=(),
            in_specs=[anywhere, anywhere],
            out_specs=[anywhere] * len(shapes),
            scratch_shapes=[pltpu.SemaphoreType.DMA((copies,))],
        ),
        out_shape=[jax.ShapeDtypeStruct(shape, lesser.dtype) for shape in shapes],
        compiler_params=pltpu.CompilerParams(vmem_limit_bytes=60 * 2**20),
        cost_estimate=pl.CostEstimate(flops=0, bytes_accessed=4 * 2**20, transcendentals=0),
        name="copied",
    )(place, lesser, greater)


def far_kernel(slot, place, offsets, pattern, bose, lesser, greater, couple, bulk, rest, total):
    cut, core = place[0], place[1]
    part = pl.program_id(0)
    energy = core if slot == 0 else 1 - core
    modes, orbitals = couple.shape[1], couple.shape[2]
    half = rest.shape[0]
    total[...] = jnp.zeros_like(total)
    for mode in range(modes):

        @pl.when((pattern[cut, mode] > 0) & (offsets[mode] == 2))
        def _():
            matrix = couple[0, mode]
            for kind, green in enumerate((lesser, greater)):
                weight = bose[mode] + jnp.where(energy == kind, 0.0, 1.0)
                left = (product(matrix, green[0, 0, 0]) * weight).astype(jnp.bfloat16)
                total[kind] += product_t(left, matrix)

    low = total[0].astype(jnp.bfloat16)
    ret = (0.5 * (total[1] - total[0])).astype(jnp.bfloat16)

    @pl.when(part == 0)
    def _():
        bulk[:orbitals] = low
        bulk[2 * orbitals : 3 * orbitals] = ret

    @pl.when(part == 1)
    def _():
        bulk[orbitals : 2 * orbitals] = low
        bulk[3 * orbitals :] = ret[: orbitals - half]
        rest[...] = ret[orbitals - half :]


def far_terms(slot, scalars, bose, lesser, greater, couplings):
    orbitals = lesser.shape[-1]
    parts = lesser.shape[2]
    modes = couplings.shape[1]
    half = orbitals // 2

    def green_at(p, place, *_):
        return (place[1] if slot == 0 else 1 - place[1], 0, p, 0, 0)

    green = pl.BlockSpec((1, 1, 1, orbitals, orbitals), green_at)
    shapes = [(4 * orbitals - half, orbitals), (half, orbitals)]
    kernel = lambda *refs: far_kernel(slot, *refs)
    return pl.pallas_call(
        kernel,
        grid_spec=pltpu.PrefetchScalarGridSpec(
            num_scalar_prefetch=4,
            grid=(parts,),
            in_specs=[
                green,
                green,
                pl.BlockSpec((1, modes, orbitals, orbitals), lambda p, *_: (0, 0, 0, 0)),
            ],
            out_specs=[pl.BlockSpec(shape, lambda p, *_: (0, 0)) for shape in shapes],
            scratch_shapes=[pltpu.VMEM((2, orbitals, orbitals), jnp.float32)],
        ),
        out_shape=[jax.ShapeDtypeStruct(shape, jnp.bfloat16) for shape in shapes],
        compiler_params=pltpu.CompilerParams(vmem_limit_bytes=32 * 2**20),
        cost_estimate=pl.CostEstimate(
            flops=parts * 2 * modes * 16 * orbitals**3, bytes_accessed=6 * 2**20, transcendentals=0
        ),
        name="far_terms",
    )(*scalars, bose, lesser, greater, couplings)


def near_kernel(
    place, offsets, pattern, bose,
    lesser, greater, first, second, inner, outer, couple, rim, low_out, ret_out, total,
):
    cut, core = place[0], place[1]
    slot = pl.program_id(1)
    energy = jnp.where(slot == 0, core, 1 - core)
    modes = couple.shape[1]
    orbitals = couple.shape[-1]
    width = rim.shape[-1]
    greens = (lesser, greater)
    total[...] = jnp.zeros_like(total)

    def wide_term(mode, arrived):
        matrix = couple[0, mode]
        for kind in range(2):
            weight = bose[mode] + jnp.where(energy == kind, 1.0, 0.0)
            left = (product(matrix, arrived[kind, 0]) * weight).astype(jnp.bfloat16)
            total[kind] += product_t(left, matrix)

    def narrow_term(mode, arrived):
        matrix = couple[0, mode]
        for kind in range(2):
            own = bose[mode] + jnp.where(energy == kind, 1.0, 0.0)
            other = bose[mode] + jnp.where(energy == kind, 0.0, 1.0)
            mixed = (
                greens[kind][0, 0, 0].astype(jnp.float32) * own
                + arrived[kind, 0].astype(jnp.float32) * other
            ).astype(jnp.bfloat16)
            left = product(matrix, mixed).astype(jnp.bfloat16)
            total[kind] += product_t(left, matrix)

    for mode in range(modes):
        here = pattern[cut, mode] > 0
        wide = offsets[mode] == 2
        for at, arrived in enumerate((first, second)):
            pl.when(here & wide & (slot != at))(lambda m=mode, a=arrived: wide_term(m, a))
            pl.when(here & ~wide & (slot == at))(lambda m=mode, a=arrived: narrow_term(m, a))

    for kind in range(2):
        for side in range(2):
            matrix = rim[0, side]
            corner = jnp.where(core == side, outer[0, kind, 0], inner[0, kind, 0])
            left = product(matrix, corner).astype(jnp.bfloat16)
            at = slice(0, width) if side == 0 else slice(orbitals - width, orbitals)
            total[kind, at, at] += product_t(left, matrix)
    low_out[0, 0] = total[0]
    ret_out[0, 0] = 0.5 * (total[1] - total[0])


def near_terms(scalars, bose, lesser, greater, near, corners, couplings, rim_couple):
    orbitals = lesser.shape[-1]
    parts = lesser.shape[2]
    modes = couplings.shape[1]
    width = rim_couple.shape[-1]

    def energy_of(j, place):
        return jnp.where(j == 0, place[1], 1 - place[1])

    own = pl.BlockSpec(
        (1, 1, 1, orbitals, orbitals), lambda p, j, place, *_: (1 - energy_of(j, place), 0, p, 0, 0)
    )
    arrived = pl.BlockSpec((2, 1, orbitals, orbitals), lambda p, j, *_: (0, p, 0, 0))
    corner = pl.BlockSpec(
        (1, 2, 1, width, width), lambda p, j, place, *_: (energy_of(j, place), 0, p, 0, 0)
    )
    out = pl.BlockSpec((1, 1, orbitals, orbitals), lambda p, j, *_: (j, p, 0, 0))
    return pl.pallas_call(
        near_kernel,
        grid_spec=pltpu.PrefetchScalarGridSpec(
            num_scalar_prefetch=4,
            grid=(parts, 2),
            in_specs=[own, own, arrived, arrived, corner, corner]
            + [
                pl.BlockSpec((1, modes, orbitals, orbitals), lambda p, j, *_: (0, 0, 0, 0)),
                pl.BlockSpec((1, 2, width, width), lambda p, j, *_: (0, 0, 0, 0)),
            ],
            out_specs=[out, out],
            scratch_shapes=[pltpu.VMEM((2, orbitals, orbitals), jnp.float32)],
        ),
        out_shape=[jax.ShapeDtypeStruct((2, parts, orbitals, orbitals), jnp.float32)] * 2,
        compiler_params=pltpu.CompilerParams(vmem_limit_bytes=32 * 2**20),
        cost_estimate=pl.CostEstimate(
            flops=parts * 4 * modes * 4 * orbitals**3, bytes_accessed=20 * 2**20, transcendentals=0
        ),
        name="near_terms",
    )(*scalars, bose, lesser, greater, *near, *corners, couplings, rim_couple)


def bulk_kernel(place, low, ret, low_first, low_second, ret_first, ret_second, low_out, ret_out):
    core = place[1]
    low_out[core, 0, 0] = (low[0, 0] + low_first[...].astype(jnp.float32)).astype(jnp.bfloat16)
    low_out[1 - core, 0, 0] = (low[1, 0] + low_second[...].astype(jnp.float32)).astype(jnp.bfloat16)

    @pl.when(pl.program_id(0) < pl.num_programs(0) - 1)
    def _():
        ret_out[core, 0, 0] = (ret[0, 0] + ret_first[...].astype(jnp.float32)).astype(jnp.bfloat16)
        ret_out[1 - core, 0, 0] = (ret[1, 0] + ret_second[...].astype(jnp.float32)).astype(jnp.bfloat16)


def bulk_added(place, low, ret, far_first, far_second):
    parts, orbitals = low.shape[1], low.shape[-1]
    rows = orbitals // 2
    steps = 2 * parts

    def low_at(c):
        return c

    def ret_at(c):
        return jnp.minimum(c, steps - 2)

    def stored(at):
        return pl.BlockSpec((2, 1, rows, orbitals), lambda c, *_: (0, at(c) // 2, at(c) % 2, 0))

    def written(at):
        return pl.BlockSpec(
            (2, 1, 1, rows, orbitals), lambda c, *_: (0, 0, at(c) // 2, at(c) % 2, 0)
        )

    low_far = pl.BlockSpec((rows, orbitals), lambda c, *_: (c, 0))
    ret_far = pl.BlockSpec((rows, orbitals), lambda c, *_: (steps + ret_at(c), 0))
    return pl.pallas_call(
        bulk_kernel,
        grid_spec=pltpu.PrefetchScalarGridSpec(
            num_scalar_prefetch=1,
            grid=(steps,),
            in_specs=[stored(low_at), stored(ret_at), low_far, low_far, ret_far, ret_far],
            out_specs=[written(low_at), written(ret_at)],
        ),
        out_shape=[jax.ShapeDtypeStruct((2, 1, parts, orbitals, orbitals), jnp.bfloat16)] * 2,
        compiler_params=pltpu.CompilerParams(vmem_limit_bytes=20 * 2**20),
        cost_estimate=pl.CostEstimate(
            flops=8 * orbitals**2, bytes_accessed=14 * 2**20, transcendentals=0
        ),
        name="bulk_added",
    )(place, low, ret, far_first, far_second, far_first, far_second)


def rest_kernel(place, ret, first, second, partial, ret_out):
    core = place[1]
    ret_out[core, 0, 0] = (ret[0, 0] + first[...].astype(jnp.float32)).astype(jnp.bfloat16)
    ret_out[1 - core, 0, 0] = (ret[1, 0] + second[...].astype(jnp.float32)).astype(jnp.bfloat16)


def rest_added(place, ret, far_first, far_second, partial):
    parts, orbitals = ret.shape[1], ret.shape[-1]
    rows = far_first.shape[0]
    last = orbitals // rows - 1
    far = pl.BlockSpec((rows, orbitals), lambda i, *_: (0, 0))
    return pl.pallas_call(
        rest_kernel,
        grid_spec=pltpu.PrefetchScalarGridSpec(
            num_scalar_prefetch=1,
            grid=(1,),
            in_specs=[
                pl.BlockSpec((2, 1, rows, orbitals), lambda i, *_: (0, parts - 1, last, 0)),
                far,
                far,
                pl.BlockSpec(memory_space=pl.ANY),
            ],
            out_specs=pl.BlockSpec(
                (2, 1, 1, rows, orbitals), lambda i, *_: (0, 0, parts - 1, last, 0)
            ),
        ),
        out_shape=jax.ShapeDtypeStruct(partial.shape, partial.dtype),
        input_output_aliases={4: 0},
        compiler_params=pltpu.CompilerParams(vmem_limit_bytes=12 * 2**20),
        cost_estimate=pl.CostEstimate(
            flops=orbitals**2, bytes_accessed=2 * 2**20, transcendentals=0
        ),
        name="rest_added",
    )(place, ret, far_first, far_second, partial)


def body(lesser, greater, couplings, rim_couple, bose_factor, offsets, pattern):
    energies = lax.axis_size("energy")
    cuts = lax.axis_size("cuts")
    orbitals = lesser.shape[-1]
    width = rim_couple.shape[-1]
    cut = lax.axis_index("cuts")
    core = cut & 1
    place = jnp.stack([cut, core]).astype(jnp.int32)
    scalars = (place, offsets, pattern)

    parts = lesser.shape[2]
    whole = (2, parts, orbitals, orbitals)
    corner = (2, 2, parts, width, width)
    cornering = functools.partial(corner_kernel, width)
    inner, outer = copied(cornering, [corner, corner], 4, place, lesser, greater)
    outer = swapped(outer, energies, cuts, False)
    near = []
    for first in (True, False):
        taking = functools.partial(near_copy_kernel, first)
        sent = copied(taking, [whole], 2, place, lesser, greater)[0]
        near.append(shifted(sent, energies, cuts, first))
    inner = swapped(inner, energies, cuts, True)

    bulk, rest = [], []
    outer, place_first = lax.optimization_barrier((outer, place))
    most, last = far_terms(0, (place_first, offsets, pattern), bose_factor, lesser, greater, couplings)
    bulk.append(shifted(most, energies, cuts, True))
    inner, place_second, last = lax.optimization_barrier((inner, place_first, last))
    rest.append(last)
    most, last = far_terms(1, (place_second, offsets, pattern), bose_factor, lesser, greater, couplings)
    bulk.append(shifted(most, energies, cuts, False))
    rest.append(last)
    near[0], near[1], rest[0], rest[1] = lax.optimization_barrier((*near, *rest))
    rest = [shifted(last, energies, cuts, slot == 0) for slot, last in enumerate(rest)]

    low, ret = near_terms(
        scalars, bose_factor, lesser, greater, near, (inner, outer), couplings, rim_couple
    )
    low_out, partial = bulk_added(place, low, ret, *bulk)
    return low_out, rest_added(place, ret, *rest, partial)


def solution(mesh):
    return jax.shard_map(
        body,
        mesh=mesh,
        in_specs=(
            P("energy", "cuts", None, None, None),
            P("energy", "cuts", None, None, None),
            P("cuts", None, None, None),
            P("cuts", None, None, None),
            P(),
            P(),
            P(),
        ),
        out_specs=(P("energy", "cuts", None, None, None), P("energy", "cuts", None, None, None)),
        check_vma=False,
    )
```

time: 123 us -> 240 us (1.95)
  Pallas kernels: 18.5 us -> 188 us
  waiting for transfers between devices: 55.7 us -> 20.7 us
  starting transfers between devices: 41.6 us -> 28.4 us
  local copies, waits for them, and re-layouts: 4.3 us -> 1.63 us
    pallas_call x2 -> x5, Pallas kernels: 5.47 us -> 153 us  [the longest x3 148 us: copied(): pl.pallas_call(kernel, grid_spec=pltpu.PrefetchScalarGridSpec(num_scalar_...]
    ppermute x2, waiting for transfers between devices: 29.8 us -> 0.01 us  [swapped(): return lax.ppermute(x, ('energy', 'cuts'), pairs)]
    ppermute x8 -> x6, starting transfers between devices: 36.3 us -> 23.9 us  [shifted(): return lax.ppermute(x, ('energy', 'cuts'), pairs)]
    pallas_call x2, Pallas kernels: 2.44 us -> 13 us  [far_terms(): pl.pallas_call(kernel, grid_spec=pltpu.PrefetchScalarGridSpec(num_scalar_...]
    pallas_call x1, Pallas kernels: 10.6 us -> 21.1 us  [near_terms(): pl.pallas_call(near_kernel, grid_spec=pltpu.PrefetchScalarGridSpec(num_sc...]
    ppermute x8 -> x6, waiting for transfers between devices: 25.8 us -> 20.7 us  [shifted(): return lax.ppermute(x, ('energy', 'cuts'), pairs)]
  transfers between devices with their start and end apart: 10 -> 8, of which waited for: 4 -> 2; matrix products, arithmetic and copies ran while one was open for 0% -> 0% of each run, Pallas kernels for 13% -> 70%
where the time goes in v2:
time: 240 us
  Pallas kernels  188 us (78%)
  starting transfers between devices  28.4 us (12%)
  waiting for transfers between devices  20.7 us (9%)
    pallas_call x3, Pallas kernels, copied(): pl.pallas_call(kernel, grid_spec=pltpu.PrefetchScalarGridSpec(num_scalar_...  148 us
    ppermute x6, starting transfers between devices, shifted(): return lax.ppermute(x, ('energy', 'cuts'), pairs)  23.9 us
    pallas_call x1, Pallas kernels, near_terms(): pl.pallas_call(near_kernel, grid_spec=pltpu.PrefetchScalarGridSpec(num_sc...  21.1 us
    ppermute x6, waiting for transfers between devices, shifted(): return lax.ppermute(x, ('energy', 'cuts'), pairs)  20.7 us
    pallas_call x2, Pallas kernels, far_terms(): pl.pallas_call(kernel, grid_spec=pltpu.PrefetchScalarGridSpec(num_scalar_...  13 us
  transfers between devices with their start and end apart: 8, of which 2 were waited for; matrix products, arithmetic and copies ran while one was open for 0% of the time, Pallas kernels for 70%

profile of v2, /device:TPU:110, one launch (start us, length us, event | category | flops | bytes accessed | tf_op | source)
XLA Modules:
  0.0 239.7 jit_solution(6443479481474803646)
XLA Ops:
  0.6 0.6 pad_add_fusion.place.refs_0_
  1.3 17.7 %copied.5 = (bf16[2,2,2,128,128]{4,3,2,1,0:T(8,128)(2,1)}, bf16[2,2,2,128,128]{4,3,2,1,0:T(8,128)(2,1)}) custom-call(s32[2]{0:T(128)} %pad_add_fusion.place.refs_0_, bf16[2,1,2,512,512]{4,3,2,1,0:T(8,128)(2,1)} %lesser.7, bf16[2,1,2,512,512]{4,3,2,1,0:T(8,128)(2,1)} %greater.7), custom_call_target="tpu_custom_call" | custom-call | bytes 4194304 | tf_op jit(solution)/shard_map/copied/pallas_call | solution.py:67
  19.0 0.7 collective-permute-start.3
  19.7 3.7 %collective-permute-start.2 = (bf16[2,2,2,128,128]{4,3,2,1,0:T(8,128)(2,1)}, bf16[2,2,2,128,128]{4,3,2,1,0:T(8,128)(2,1)}, u32[]{:S(2)}, u32[]{:S(2)}) collective-permute-start(bf16[2,2,2,128,128]{4,3,2,1,0:T(8,128)(2,1)} %get-tuple-element.21), channel_id=1, source_target_pairs={{0,1},{1,0},{2,3},{3,2},{4,5},{5,4},{6,7},{7,6},{8,9},{9,8},{10,11... | collective-permute-start | bytes 786440 | tf_op jit(solution)/shard_map/ppermute | solution.py:18
  23.4 65.3 %copied.3 = bf16[2,2,512,512]{3,2,1,0:T(8,128)(2,1)} custom-call(s32[2]{0:T(128)} %pad_add_fusion.place.refs_0_, bf16[2,1,2,512,512]{4,3,2,1,0:T(8,128)(2,1)} %lesser.7, bf16[2,1,2,512,512]{4,3,2,1,0:T(8,128)(2,1)} %greater.7), custom_call_target="tpu_custom_call" | custom-call | bytes 4194304 | tf_op jit(solution)/shard_map/copied/pallas_call | solution.py:67
  88.7 0.0 copy-start
  88.7 0.0 copy-start.2
  88.7 0.0 copy-start.3
  88.7 0.0 copy-start.5
  88.8 0.0 copy-start.6
  88.8 0.0 copy-start.7
  88.8 6.0 %collective-permute-start = (bf16[2,2,512,512]{3,2,1,0:T(8,128)(2,1)}, bf16[2,2,512,512]{3,2,1,0:T(8,128)(2,1)}, u32[]{:S(2)}, u32[]{:S(2)}) collective-permute-start(bf16[2,2,512,512]{3,2,1,0:T(8,128)(2,1)} %copied.3), channel_id=1, source_target_pairs={{0,4},{2,6},{4,8},{5,1},{6,10},{7,3},{8,12},{9,5},{10,14},{11,7},{... | collective-permute-start | bytes 6291464 | tf_op jit(solution)/shard_map/ppermute | solution.py:29
  94.8 65.3 %copied.4 = bf16[2,2,512,512]{3,2,1,0:T(8,128)(2,1)} custom-call(s32[2]{0:T(128)} %pad_add_fusion.place.refs_0_, bf16[2,1,2,512,512]{4,3,2,1,0:T(8,128)(2,1)} %lesser.7, bf16[2,1,2,512,512]{4,3,2,1,0:T(8,128)(2,1)} %greater.7), custom_call_target="tpu_custom_call" | custom-call | bytes 4194304 | tf_op jit(solution)/shard_map/copied/pallas_call | solution.py:67
  160.1 1.9 collective-permute-start.1
  162.0 0.0 collective-permute-done.3.outer
  162.0 0.0 copy-done
  162.1 0.0 copy-done.2
  162.1 0.0 copy-done.3
  162.1 0.0 copy-done.5
  162.1 0.0 copy-done.6
  162.1 0.0 copy-done.7
  162.1 0.0 copy-start.1
  162.1 1.6 copy-done.1
  163.7 6.5 %far_terms.2 = (bf16[1792,512]{1,0:T(8,128)(2,1)S(1)}, bf16[256,512]{1,0:T(8,128)(2,1)S(1)}) custom-call(s32[2]{0:T(128)S(1)} %copy-done.2, s32[3]{0:T(128)S(1)} %copy-done.6, s32[4,3]{1,0:T(4,128)S(1)} %copy-done.5, f32[3]{0:T(128)S(1)} %copy-done.7, bf16[2,1,2,512,512]{4,3,2,1,0:T(8,128)(2,1)S(1)} %copy-done, bf16[2,1,2,512,512]{4,3,2,1,0:T(8,128)(2,1)S(1)} %copy-done.1, ...), custom_call_target="tpu_custom_call" | custom-call | flops 25769803776 | bytes 6291456 | tf_op jit(solution)/shard_map/far_terms/pallas_call | solution.py:127
  170.2 0.0 collective-permute-done.2.inner
  170.2 0.0 copy-start.4
  170.2 8.3 %collective-permute-start.4 = (bf16[1792,512]{1,0:T(8,128)(2,1)S(1)}, bf16[1792,512]{1,0:T(8,128)(2,1)S(1)}, u32[]{:S(2)}, u32[]{:S(2)}) collective-permute-start(bf16[1792,512]{1,0:T(8,128)(2,1)S(1)} %get-tuple-element.34), channel_id=1, source_target_pairs={{0,4},{2,6},{4,8},{5,1},{6,10},{7,3},{8,12},{9,5},{10,14},{11,7},{... | collective-permute-start | bytes 5505032 | tf_op jit(solution)/shard_map/ppermute | solution.py:29
  178.5 6.5 %far_terms.3 = (bf16[1792,512]{1,0:T(8,128)(2,1)S(1)}, bf16[256,512]{1,0:T(8,128)(2,1)S(1)}) custom-call(s32[2]{0:T(128)S(1)} %copy-done.2, s32[3]{0:T(128)S(1)} %copy-done.6, s32[4,3]{1,0:T(4,128)S(1)} %copy-done.5, f32[3]{0:T(128)S(1)} %copy-done.7, bf16[2,1,2,512,512]{4,3,2,1,0:T(8,128)(2,1)S(1)} %copy-done, bf16[2,1,2,512,512]{4,3,2,1,0:T(8,128)(2,1)S(1)} %copy-done.1, ...), custom_call_target="tpu_custom_call" | custom-call | flops 25769803776 | bytes 6291456 | tf_op jit(solution)/shard_map/far_terms/pallas_call | solution.py:127
  185.0 1.9 collective-permute-start.5
  187.0 0.0 collective-permute-done.first
  187.0 19.5 %collective-permute-done.1.second = bf16[2,2,512,512]{3,2,1,0:T(8,128)(2,1)S(1)} collective-permute-done((bf16[2,2,512,512]{3,2,1,0:T(8,128)(2,1)}, bf16[2,2,512,512]{3,2,1,0:T(8,128)(2,1)S(1)}, u32[]{:S(2)}, u32[]{:S(2)}) %collective-permute-start.1) | collective-permute-done | bytes 2097184 | tf_op jit(solution)/shard_map/ppermute | solution.py:29
  206.5 1.9 collective-permute-start.6
  208.4 3.9 %collective-permute-start.7 = (bf16[256,512]{1,0:T(8,128)(2,1)S(1)}, bf16[256,512]{1,0:T(8,128)(2,1)S(1)}, u32[]{:S(2)}, u32[]{:S(2)}) collective-permute-start(bf16[256,512]{1,0:T(8,128)(2,1)S(1)} %get-tuple-element.38), channel_id=1, source_target_pairs={{1,5},{3,7},{4,0},{5,9},{6,2},{7,11},{8,4},{9,13},{10,6},{11,15},{... | collective-permute-start | bytes 786440 | tf_op jit(solution)/shard_map/ppermute | solution.py:29
  212.3 0.0 copy-done.4
  212.3 21.1 %near_terms.1 = (f32[2,2,512,512]{3,2,1,0:T(8,128)S(1)}, f32[2,2,512,512]{3,2,1,0:T(8,128)S(1)}) custom-call(s32[2]{0:T(128)S(1)} %copy-done.2, s32[3]{0:T(128)S(1)} %copy-done.6, s32[4,3]{1,0:T(4,128)S(1)} %copy-done.5, f32[3]{0:T(128)S(1)} %copy-done.7, bf16[2,1,2,512,512]{4,3,2,1,0:T(8,128)(2,1)S(1)} %copy-done, ...), custom_call_target="tpu_custom_call" | custom-call | flops 12884901888 | bytes 20971520 | tf_op jit(solution)/shard_map/near_terms/pallas_call | solution.py:216
  233.4 0.0 collective-permute-done.4.low_first.ret_first
  233.4 1.2 collective-permute-done.5.low_second.ret_second
  234.6 3.7 %bulk_added.1 = (bf16[2,1,2,512,512]{4,3,2,1,0:T(8,128)(2,1)}, bf16[2,1,2,512,512]{4,3,2,1,0:T(8,128)(2,1)}) custom-call(s32[2]{0:T(128)S(1)} %copy-done.2, f32[2,2,512,512]{3,2,1,0:T(8,128)S(1)} %get-tuple-element.32.low, f32[2,2,512,512]{3,2,1,0:T(8,128)S(1)} %get-tuple-element.33.ret, bf16[1792,512]{1,0:T(8,128)(2,1)S(1)} %collective-permute-done.4.low_first.ret_first, ...), custom_call_target="tpu_custom_call" | custom-call | flops 2097152 | bytes 14680064 | tf_op jit(solution)/shard_map/bulk_added/pallas_call | solution.py:270
  238.3 0.0 collective-permute-done.6.first
  238.3 0.0 collective-permute-done.7.second
  238.3 1.4 rest_added.1
Async XLA Ops:
  19.0 143.1 %collective-permute-start.3 = (bf16[2,2,2,128,128]{4,3,2,1,0:T(8,128)(2,1)}, bf16[2,2,2,128,128]{4,3,2,1,0:T(8,128)(2,1)S(1)}, u32[]{:S(2)}, u32[]{:S(2)}) collective-permute-start(bf16[2,2,2,128,128]{4,3,2,1,0:T(8,128)(2,1)} %get-tuple-element.22), channel_id=1, source_target_pairs={{1,2},{2,1},{5,6},{6,5},{9,10},{10,9},{13,14},{14,13},{17,18},{18,... | collective-permute-start | bytes 786440 | tf_op jit(solution)/shard_map/ppermute | solution.py:18
  19.7 150.6 %collective-permute-start.2 = (bf16[2,2,2,128,128]{4,3,2,1,0:T(8,128)(2,1)}, bf16[2,2,2,128,128]{4,3,2,1,0:T(8,128)(2,1)}, u32[]{:S(2)}, u32[]{:S(2)}) collective-permute-start(bf16[2,2,2,128,128]{4,3,2,1,0:T(8,128)(2,1)} %get-tuple-element.21), channel_id=1, source_target_pairs={{0,1},{1,0},{2,3},{3,2},{4,5},{5,4},{6,7},{7,6},{8,9},{9,8},{10,11... | collective-permute-start | bytes 786440 | tf_op jit(solution)/shard_map/ppermute | solution.py:18
  88.7 73.3 %copy-start = (bf16[2,1,2,512,512]{4,3,2,1,0:T(8,128)(2,1)S(1)}, bf16[2,1,2,512,512]{4,3,2,1,0:T(8,128)(2,1)}, u32[]{:S(2)}) copy-start(bf16[2,1,2,512,512]{4,3,2,1,0:T(8,128)(2,1)} %lesser.7) | copy-start | bytes 6291460
  88.7 73.3 %copy-start.2 = (s32[2]{0:T(128)S(1)}, s32[2]{0:T(128)}, u32[]{:S(2)}) copy-start(s32[2]{0:T(128)} %pad_add_fusion.place.refs_0_) | copy-start | bytes 28
  88.7 73.3 %copy-start.3 = (bf16[1,3,512,512]{3,2,1,0:T(8,128)(2,1)S(1)}, bf16[1,3,512,512]{3,2,1,0:T(8,128)(2,1)}, u32[]{:S(2)}) copy-start(bf16[1,3,512,512]{3,2,1,0:T(8,128)(2,1)} %couple.1) | copy-start | bytes 4718596
  88.7 73.3 %copy-start.5 = (s32[4,3]{1,0:T(4,128)S(1)}, s32[4,3]{1,0:T(4,128)}, u32[]{:S(2)}) copy-start(s32[4,3]{1,0:T(4,128)} %pattern.1) | copy-start | bytes 148
  88.8 73.3 %copy-start.6 = (s32[3]{0:T(128)S(1)}, s32[3]{0:T(128)}, u32[]{:S(2)}) copy-start(s32[3]{0:T(128)} %offsets.1) | copy-start | bytes 40
  88.8 73.3 %copy-start.7 = (f32[3]{0:T(128)S(1)}, f32[3]{0:T(128)}, u32[]{:S(2)}) copy-start(f32[3]{0:T(128)} %bose.1) | copy-start | bytes 40
  88.8 98.2 %collective-permute-start = (bf16[2,2,512,512]{3,2,1,0:T(8,128)(2,1)}, bf16[2,2,512,512]{3,2,1,0:T(8,128)(2,1)}, u32[]{:S(2)}, u32[]{:S(2)}) collective-permute-start(bf16[2,2,512,512]{3,2,1,0:T(8,128)(2,1)} %copied.3), channel_id=1, source_target_pairs={{0,4},{2,6},{4,8},{5,1},{6,10},{7,3},{8,12},{9,5},{10,14},{11,7},{... | collective-permute-start | bytes 6291464 | tf_op jit(solution)/shard_map/ppermute | solution.py:29
  160.1 46.4 %collective-permute-start.1 = (bf16[2,2,512,512]{3,2,1,0:T(8,128)(2,1)}, bf16[2,2,512,512]{3,2,1,0:T(8,128)(2,1)S(1)}, u32[]{:S(2)}, u32[]{:S(2)}) collective-permute-start(bf16[2,2,512,512]{3,2,1,0:T(8,128)(2,1)} %copied.4), channel_id=1, source_target_pairs={{1,5},{3,7},{4,0},{5,9},{6,2},{7,11},{8,4},{9,13},{10,6},{11,15},{... | collective-permute-start | bytes 6291464 | tf_op jit(solution)/shard_map/ppermute | solution.py:29
  162.1 1.6 copy-start.1
  170.2 42.1 %copy-start.4 = (bf16[1,2,128,128]{3,2,1,0:T(8,128)(2,1)S(1)}, bf16[1,2,128,128]{3,2,1,0:T(8,128)(2,1)}, u32[]{:S(2)}) copy-start(bf16[1,2,128,128]{3,2,1,0:T(8,128)(2,1)} %rim.1) | copy-start | bytes 196612
  170.2 63.2 %collective-permute-start.4 = (bf16[1792,512]{1,0:T(8,128)(2,1)S(1)}, bf16[1792,512]{1,0:T(8,128)(2,1)S(1)}, u32[]{:S(2)}, u32[]{:S(2)}) collective-permute-start(bf16[1792,512]{1,0:T(8,128)(2,1)S(1)} %get-tuple-element.34), channel_id=1, source_target_pairs={{0,4},{2,6},{4,8},{5,1},{6,10},{7,3},{8,12},{9,5},{10,14},{11,7},{... | collective-permute-start | bytes 5505032 | tf_op jit(solution)/shard_map/ppermute | solution.py:29
  185.0 49.5 %collective-permute-start.5 = (bf16[1792,512]{1,0:T(8,128)(2,1)S(1)}, bf16[1792,512]{1,0:T(8,128)(2,1)S(1)}, u32[]{:S(2)}, u32[]{:S(2)}) collective-permute-start(bf16[1792,512]{1,0:T(8,128)(2,1)S(1)} %get-tuple-element.35), channel_id=1, source_target_pairs={{1,5},{3,7},{4,0},{5,9},{6,2},{7,11},{8,4},{9,13},{10,6},{11,15},{... | collective-permute-start | bytes 5505032 | tf_op jit(solution)/shard_map/ppermute | solution.py:29
  206.5 31.8 %collective-permute-start.6 = (bf16[256,512]{1,0:T(8,128)(2,1)S(1)}, bf16[256,512]{1,0:T(8,128)(2,1)S(1)}, u32[]{:S(2)}, u32[]{:S(2)}) collective-permute-start(bf16[256,512]{1,0:T(8,128)(2,1)S(1)} %get-tuple-element.37), channel_id=1, source_target_pairs={{0,4},{2,6},{4,8},{5,1},{6,10},{7,3},{8,12},{9,5},{10,14},{11,7},{... | collective-permute-start | bytes 786440 | tf_op jit(solution)/shard_map/ppermute | solution.py:29
  208.4 29.9 %collective-permute-start.7 = (bf16[256,512]{1,0:T(8,128)(2,1)S(1)}, bf16[256,512]{1,0:T(8,128)(2,1)S(1)}, u32[]{:S(2)}, u32[]{:S(2)}) collective-permute-start(bf16[256,512]{1,0:T(8,128)(2,1)S(1)} %get-tuple-element.38), channel_id=1, source_target_pairs={{1,5},{3,7},{4,0},{5,9},{6,2},{7,11},{8,4},{9,13},{10,6},{11,15},{... | collective-permute-start | bytes 786440 | tf_op jit(solution)/shard_map/ppermute | solution.py:29
